TPU v7x, 512 devices: a whole 4x4x16 slice. The times are simulated.
512 devices in a mesh: sub: 8 (over y, z_hi), row: 8 (over z_lo), col: 8 (over x, core).
Axes of the slice: x: 4, y: 4, z: 16 (z_hi: 2, z_lo: 8; z = z_hi * 8 + z_lo), core: 2. Of those that a mesh axis runs over, the one named last changes fastest.
Arguments:
- root_inverse: float32 [8192, 8192], P(('sub', 'row'), 'col')
- panel: float32 [8192, 2048], P(('sub', 'row'), 'col'), may hold values from -0.125 to 0.125
- pattern: int32 [64, 16], P(('sub', 'row'), 'col'), may hold values from 0 to 1, as said below
- diag_inverse: float32 [2048, 2048], P(('sub', 'row'), 'col')
Outputs:
- off_block: float32 [8192, 2048], P(('sub', 'row'), 'col')
- diag_block: float32 [2048, 2048], P(('sub', 'row'), 'col')
Inputs may be any that keep to these rules, and one draw needn't show every extreme that they name: `pattern`: in every tile row, each aligned group of 2 tile columns (those of one index of col) has exactly one tile marked 1.
All inputs are finite; a program needn't handle non-finite values.
Results may differ from a plain program's by a relative error of at most 0.000078.
Values sent between devices are 32-bit elements; how exact they have to be, the bound alone decides.
A program may use at most 64 MiB of HBM per device.

v0:
```python
import jax
import jax.numpy as jnp
from jax import lax
from jax.sharding import PartitionSpec as P

highest = lax.Precision.HIGHEST


def rows_of_inverse(root_inverse):
    return lax.all_gather(root_inverse, "col", axis=1, tiled=True)


def local(root_inverse, panel, pattern, diag_inverse):
    tile_rows = panel.shape[0]
    marked = pattern[0].astype(jnp.float32)
    column_mask = jnp.repeat(marked, tile_rows)
    masked_panel = panel * column_mask[None, :]
    inverse_full = rows_of_inverse(root_inverse)
    accumulated = jnp.dot(
        inverse_full,
        lax.all_gather(masked_panel, ("sub", "row"), axis=0, tiled=True),
        precision=highest,
        preferred_element_type=jnp.float32,
    )
    off_block = -(accumulated * column_mask[None, :])
    panel_full_row = lax.all_gather(masked_panel, "col", axis=1, tiled=True)
    contribution = lax.dot_general(
        panel_full_row,
        off_block,
        (((0,), (0,)), ((), ())),
        precision=highest,
        preferred_element_type=jnp.float32,
    )
    update = lax.psum_scatter(contribution, ("sub", "row"), scatter_dimension=0, tiled=True)
    diag_block = diag_inverse - update
    return (off_block, diag_block)


def solution(mesh):
    in_specs = (
        P(("sub", "row"), "col"),
        P(("sub", "row"), "col"),
        P(("sub", "row"), "col"),
        P(("sub", "row"), "col"),
    )
    out_specs = (P(("sub", "row"), "col"), P(("sub", "row"), "col"))
    return jax.shard_map(local, mesh=mesh, in_specs=in_specs, out_specs=out_specs, check_vma=False)
```

profile of v0, /device:TPU:2, one launch (start us, length us, event | category | flops | bytes accessed | tf_op | source)
XLA Modules:
  0.0 950.3 jit_solution(14879854118065150119)
XLA Ops:
  7.2 0.0 all-gather.6.cloned.1.call-start
  7.2 0.7 all-gather.6.cloned.1.call-update
  7.9 0.0 all-gather.4.cloned.1.call-start
  7.9 0.7 convert_bitcast_fusion
  8.6 0.1 broadcast_bitcast_fusion
  8.7 1.6 broadcast_multiply_fusion
  10.2 0.0 all-gather.4.cloned.1.call-update
  10.3 0.0 all-gather.8.cloned.1.call-start
  10.3 0.7 all-gather.8.cloned.1.call-update
  11.0 0.0 reduce-scatter.2.cloned.1.call-start
  11.1 42.3 %all-gather.6.cloned.1.call-done = f32[128,8192]{1,0:T(8,128)} async-done(((f32[128,1024]{1,0:T(8,128)}), f32[128,8192]{1,0:T(8,128)}) %all-gather.6.cloned.1.call-update) | async-done | bytes 4194320 | tf_op jit(solution)/shard_map/all_gather | solution.py:10
  53.4 161.6 %all-gather.4.cloned.1.call-done = f32[8192,256]{1,0:T(8,128)} async-done(((f32[128,256]{1,0:T(8,128)}), f32[8192,256]{1,0:T(8,128)}) %all-gather.4.cloned.1.call-update) | async-done | bytes 8388624 | tf_op jit(solution)/shard_map/all_gather | solution.py:21
  215.0 16.3 %fusion = f32[256,128]{1,0:T(8,128)S(1)} fusion(f32[8192,256]{1,0:T(8,128)} %all-gather.4.cloned.1.call-done, f32[128,8192]{1,0:T(8,128)} %all-gather.6.cloned.1.call-done, f32[256]{0:T(256)S(1)} %broadcast_bitcast_fusion), kind=kOutput, calls=%fused_computation.1 | convolution fusion | flops 3221291008 | bytes 12715008 | tf_op jit(solution)/shard_map/dot_general | solution.py:19
  231.3 0.0 copy-start
  231.3 11.0 %all-gather.8.cloned.1.call-done = f32[128,2048]{1,0:T(8,128)} async-done(((f32[128,256]{1,0:T(8,128)}), f32[128,2048]{1,0:T(8,128)}) %all-gather.8.cloned.1.call-update) | async-done | bytes 1048592 | tf_op jit(solution)/shard_map/all_gather | solution.py:26
  242.3 4.4 fusion.1
  246.7 0.0 reduce-scatter.2.cloned.1.call-update
  246.7 0.8 copy.6
  247.5 694.9 %reduce-scatter.2.cloned.1.call-done = f32[32,256]{1,0:T(8,128)} async-done(((f32[2048,256]{1,0:T(8,128)}), f32[32,256]{1,0:T(8,128)}) %reduce-scatter.2.cloned.1.call-update) | async-done | bytes 32784 | tf_op jit(solution)/shard_map/reduce_scatter | solution.py:34
  942.4 0.0 copy-done
  942.4 1.4 sub.3
Async XLA Ops:
  7.2 46.2 %all-gather.6.cloned.1.call-start = ((), (), s32[]{:S(2)}) async-start(), calls=%async_computation.2 | async-start | bytes 4718592 | tf_op jit(solution)/shard_map/all_gather | solution.py:10
  7.9 207.1 %all-gather.4.cloned.1.call-start = ((), (), s32[]{:S(2)}) async-start(), calls=%async_computation.1 | async-start | bytes 8519680 | tf_op jit(solution)/shard_map/all_gather | solution.py:21
  10.3 232.0 %all-gather.8.cloned.1.call-start = ((), (), s32[]{:S(2)}) async-start(), calls=%async_computation.3 | async-start | bytes 1179648 | tf_op jit(solution)/shard_map/all_gather | solution.py:26
  11.0 931.4 %reduce-scatter.2.cloned.1.call-start = ((), (), s32[]{:S(2)}) async-start(), calls=%async_computation.4 | async-start | bytes 2129920 | tf_op jit(solution)/shard_map/reduce_scatter | solution.py:34
  231.3 711.1 %copy-start = (f32[32,256]{1,0:T(8,128)S(1)}, f32[32,256]{1,0:T(8,128)}, u32[]{:S(2)}) copy-start(f32[32,256]{1,0:T(8,128)} %param.7) | copy-start | bytes 98308
Sparse Core Ops, SparseCore 0:
  10.1 43.1 all-gather.5
  56.9 158.0 all-gather.3
  217.7 24.5 all-gather.7
  246.8 695.4 reduce-scatter.1
where the time goes:
time: 951 us; the launch traced here: 950 us
  waiting for transfers between devices  911 us (96%)
  matrix products  20.7 us (2%)
  between operations  13.8 us (1%)
    reduce_scatter x1, waiting for transfers between devices, local(): lax.psum_scatter(contribution, ('sub', 'row'), scatter_dimension=0, tiled...  695 us
    all_gather x1, waiting for transfers between devices, local(): lax.all_gather(masked_panel, ('sub', 'row'), axis=0, tiled=True)  162 us
    all_gather x1, waiting for transfers between devices, rows_of_inverse(): return lax.all_gather(root_inverse, 'col', axis=1, tiled=True)  42.3 us
  transfers between devices with their start and end apart: 4, of which 4 were waited for; matrix products, arithmetic and copies ran while one was open for 2% of the time, Pallas kernels for 0%

commit v1 on v0

--- a/solution.py
+++ b/solution.py
@@ -2,12 +2,41 @@
 import jax.numpy as jnp
 from jax import lax
 from jax.sharding import PartitionSpec as P
+from jax.lax import axis_index, axis_size, ppermute
 
 highest = lax.Precision.HIGHEST
 
 
+def close_edges(inner_x, array_axis):
+    inner_x = jnp.moveaxis(inner_x, 0, array_axis)
+    mixed_arr = inner_x.shape
+    return inner_x.reshape(
+        *mixed_arr[:array_axis],
+        mixed_arr[array_axis] * mixed_arr[array_axis + 1],
+        *mixed_arr[array_axis + 2 :]
+    )
+
+
+def widths_process(row_dim, u, net_axis):
+    how_many = axis_size(net_axis)
+    windows = [(dev_j, (dev_j + 1) % how_many) for dev_j in range(how_many)]
+    all_blocks = [(m, k) for k, m in windows]
+    right_arr, block_last = ([], [])
+    idx = 0
+    while idx < how_many - 1:
+        if idx % 2 == 0:
+            right_arr.append(ppermute(right_arr[-1] if right_arr else u, net_axis, windows))
+        else:
+            block_last.append(ppermute(block_last[-1] if block_last else u, net_axis, all_blocks))
+        idx += 1
+    next_value = jnp.stack([*right_arr[::-1], u, *block_last], axis=0)
+    block_now = axis_index(net_axis) - len(right_arr)
+    next_value = next_value[(jnp.arange(how_many) - block_now) % how_many]
+    return close_edges(next_value, row_dim)
+
+
 def rows_of_inverse(root_inverse):
-    return lax.all_gather(root_inverse, "col", axis=1, tiled=True)
+    return widths_process(1, root_inverse, "col")
 
 
 def local(root_inverse, panel, pattern, diag_inverse):

time: 951 us -> 908 us (0.955)
  the two profiles are of different devices: /device:TPU:2 before, /device:TPU:4 now
where the time goes in v1:
time: 908 us; the launch traced here: 907 us
  waiting for transfers between devices  850 us (94%)
  local copies, waits for them, and re-layouts  18.3 us (2%)
  matrix products  15.9 us (2%)
  between operations  13.8 us (2%)
    reduce_scatter x1, waiting for transfers between devices, local(): lax.psum_scatter(contribution, ('sub', 'row'), scatter_dimension=0, tiled...  695 us
    all_gather x1, waiting for transfers between devices, local(): lax.all_gather(masked_panel, ('sub', 'row'), axis=0, tiled=True)  110 us
    ppermute x4, waiting for transfers between devices, widths_process(): ppermute(right_arr[-1] if right_arr else u, net_axis, windows)  28.7 us
  transfers between devices with their start and end apart: 10, of which 8 were waited for; matrix products, arithmetic and copies ran while one was open for 3% of the time, Pallas kernels for 0%

profile of v1, /device:TPU:4, one launch (start us, length us, event | category | flops | bytes accessed | tf_op | source)
XLA Modules:
  0.0 907.2 jit_solution(11375981855370127096)
XLA Ops:
  7.2 0.0 copy-start.1
  7.2 0.0 all-gather.3.cloned.1.call-start
  7.2 0.7 convert_bitcast_fusion
  7.9 0.1 broadcast_bitcast_fusion
  8.0 1.6 broadcast_multiply_fusion
  9.6 0.0 all-gather.3.cloned.1.call-update
  9.6 0.0 all-gather.5.cloned.1.call-start
  9.7 0.0 collective-permute-start
  9.7 8.8 collective-permute-done
  18.5 0.0 collective-permute-start.1
  18.5 1.7 collective-permute-start.4
  20.2 6.9 collective-permute-done.1
  27.1 0.0 collective-permute-start.2
  27.1 0.2 collective-permute-done.4
  27.2 1.8 collective-permute-start.5
  29.0 6.6 collective-permute-done.2
  35.7 0.0 collective-permute-start.3
  35.7 0.0 all-gather.5.cloned.1.call-update
  35.7 0.0 reduce-scatter.2.cloned.1.call-start
  35.8 0.0 collective-permute-done.5
  35.8 2.2 collective-permute-start.6
  38.0 6.4 collective-permute-done.3
  44.4 1.9 bitcast_dynamic-update-slice_fusion.7
  46.3 0.9 bitcast_dynamic-update-slice_fusion.6
  47.2 0.8 bitcast_dynamic-update-slice_fusion.5
  48.0 0.9 bitcast_dynamic-update-slice_fusion.4
  48.9 0.0 copy-done.1
  48.9 0.8 bitcast_dynamic-update-slice_fusion.3
  49.7 0.8 bitcast_dynamic-update-slice_fusion.2
  50.6 0.8 bitcast_dynamic-update-slice_fusion.1
  51.4 0.0 collective-permute-done.6
  51.4 0.8 bitcast_dynamic-update-slice_fusion
  52.2 5.0 gather_fusion
  57.2 5.4 copy.6
  62.6 109.8 %all-gather.3.cloned.1.call-done = f32[8192,256]{1,0:T(8,128)} async-done(((f32[128,256]{1,0:T(8,128)}), f32[8192,256]{1,0:T(8,128)}) %all-gather.3.cloned.1.call-update) | async-done | bytes 8388624 | tf_op jit(solution)/shard_map/all_gather | solution.py:50
  172.4 11.5 %fusion = f32[128,256]{1,0:T(8,128)S(1)} fusion(f32[128,8192]{0,1:T(8,128)} %bitcast.28, f32[8192,256]{1,0:T(8,128)} %all-gather.3.cloned.1.call-done, f32[256]{0:T(256)S(1)} %broadcast_bitcast_fusion), kind=kOutput, calls=%fused_computation.2 | convolution fusion | flops 3221291008 | bytes 12715008 | tf_op jit(solution)/shard_map/dot_general | solution.py:48
  183.9 0.0 copy-start
  183.9 0.0 copy-start.2
  183.9 15.5 %all-gather.5.cloned.1.call-done = f32[128,2048]{1,0:T(8,128)} async-done(((f32[128,256]{1,0:T(8,128)}), f32[128,2048]{1,0:T(8,128)}) %all-gather.5.cloned.1.call-update) | async-done | bytes 1048592 | tf_op jit(solution)/shard_map/all_gather | solution.py:55
  199.4 4.4 fusion.3
  203.8 0.0 reduce-scatter.2.cloned.1.call-update
  203.8 695.5 %reduce-scatter.2.cloned.1.call-done = f32[32,256]{1,0:T(8,128)} async-done(((f32[2048,256]{1,0:T(8,128)}), f32[32,256]{1,0:T(8,128)}) %reduce-scatter.2.cloned.1.call-update) | async-done | bytes 32784 | tf_op jit(solution)/shard_map/reduce_scatter | solution.py:63
  899.3 0.0 copy-done.2
  899.3 1.4 sub.22
  900.7 0.0 copy-done
  (2 shorter events, 0.0 us)
Async XLA Ops:
  7.2 41.7 %copy-start.1 = (f32[128,1024]{1,0:T(8,128)S(1)}, f32[128,1024]{1,0:T(8,128)}, u32[]{:S(2)}) copy-start(f32[128,1024]{1,0:T(8,128)} %param.4) | copy-start | bytes 1572868
  7.2 165.2 %all-gather.3.cloned.1.call-start = ((), (), s32[]{:S(2)}) async-start(), calls=%async_computation.1 | async-start | bytes 8519680 | tf_op jit(solution)/shard_map/all_gather | solution.py:50
  9.6 189.8 %all-gather.5.cloned.1.call-start = ((), (), s32[]{:S(2)}) async-start(), calls=%async_computation.2 | async-start | bytes 1179648 | tf_op jit(solution)/shard_map/all_gather | solution.py:55
  9.7 8.8 collective-permute-start
  18.5 8.6 collective-permute-start.1
  18.5 8.8 collective-permute-start.4
  27.1 8.6 collective-permute-start.2
  27.2 8.6 collective-permute-start.5
  35.7 8.7 collective-permute-start.3
  35.7 863.6 %reduce-scatter.2.cloned.1.call-start = ((), (), s32[]{:S(2)}) async-start(), calls=%async_computation.3 | async-start | bytes 2129920 | tf_op jit(solution)/shard_map/reduce_scatter | solution.py:63
  35.8 15.6 %collective-permute-start.6 = (f32[128,1024]{1,0:T(8,128)S(1)}, f32[128,1024]{1,0:T(8,128)S(1)}, u32[]{:S(2)}, u32[]{:S(2)}) collective-permute-start(f32[128,1024]{1,0:T(8,128)S(1)} %collective-permute-done.5), channel_id=1, source_target_pairs={{1,0},{2,1},{3,2},{4,3},{5,4},{6,5},{7,6},{0,7},{9,8},{10,9},{11,1... | collective-permute-start | bytes 1572872 | tf_op jit(solution)/shard_map/ppermute | solution.py:30
  183.9 716.7 %copy-start = (f32[128,256]{1,0:T(8,128)}, f32[128,256]{1,0:T(8,128)S(1)}, u32[]{:S(2)}) copy-start(f32[128,256]{1,0:T(8,128)S(1)} %fusion) | copy-start | bytes 393220
  183.9 715.3 %copy-start.2 = (f32[32,256]{1,0:T(8,128)S(1)}, f32[32,256]{1,0:T(8,128)}, u32[]{:S(2)}) copy-start(f32[32,256]{1,0:T(8,128)} %param.7) | copy-start | bytes 98308
Sparse Core Ops, SparseCore 0:
  11.0 161.3 all-gather.2
  174.5 24.8 all-gather.4
  203.9 695.2 reduce-scatter.1
